TPU v7x, 256 devices: a whole 4x4x8 slice. The times are simulated.
256 devices in a mesh: seq: 32 (over x, z), head: 8 (over y, core).
Axes of the slice: x: 4, y: 4, z: 8, core: 2. Of those that a mesh axis runs over, the one named last changes fastest.
Arguments:
- latent_cache: bfloat16 [2048, 64, 576], P('seq'), may hold values from -6 to 6
- block_owner: int32 [2048], P('seq'), may hold values from 0 to 15, as said below
- block_index: int32 [2048], P('seq'), may hold values from 0 to 1016, as said below
- cache_lengths: int32 [16], replicated, may hold values from 1 to 65088, as said below
- query_nope: bfloat16 [2, 16, 128, 128], P(None, None, 'head'), may hold values from -6 to 6
- query_rope: bfloat16 [2, 16, 128, 64], P(None, None, 'head'), may hold values from -136 to 136
- new_latent: bfloat16 [2, 16, 576], replicated, may hold values from -6 to 6
- w_uk: bfloat16 [128, 128, 512], P('head'), may hold values from -0.25 to 0.25
- value_up_weight: bfloat16 [128, 512, 128], P('head'), may hold values from -0.25 to 0.25
- w_out: bfloat16 [16384, 7168], P('head', 'seq'), may hold values from -0.1875 to 0.1875
Outputs:
- attended: bfloat16 [16, 2, 7168], P('head', None, 'seq')
Inputs may be any that keep to these rules, and one draw needn't show every extreme that they name: `block_owner`: every request owns at least one block; request r owns exactly ceil(cache_lengths[r] / 64) blocks, whose block_index values are 0 up to that count minus one. `block_index`: together with block_owner, names each block of each request exactly once; one request owns exactly (1017) blocks, no request more. `cache_lengths`: the blocks of all requests fill all 2048 slots.
All inputs are finite; a program needn't handle non-finite values.
Results may differ from a plain program's by a relative error of at most 0.015.
Values may be sent and summed in bfloat16 or wider, within the bound.
No kernel may reach another device: no remote copies, remote signals or barrier semaphores. Data moves between devices by JAX's collectives and lax.ppermute only.
A program may use at most 192 MiB of HBM per device.

v0:
```python
import jax
import jax.numpy as jnp
from jax import lax
from jax.sharding import PartitionSpec as P

KVL = 512
ROPE = 64
NOPE = 128
VD = 128
BLK = 64


NEG = -1e30


def joined(value, axis, join):
    pieces = jax.tree.map(lambda part: lax.all_gather(part, axis), value)
    head = jax.tree.map(lambda part: part[0], pieces)
    tail = jax.tree.map(lambda part: part[1:], pieces)
    subtotal, _ = lax.scan(lambda subtotal, piece: (join(subtotal, piece), None), head, tail)
    return subtotal


def finish(m, l, acc, q_items, keys, step_of):
    steps = keys.shape[1]
    s = jnp.einsum("kc,kjc->kj", q_items, keys, preferred_element_type=jnp.float32) * (
        NOPE + ROPE
    ) ** (-0.5)
    live = jnp.arange(steps)[None, :] <= step_of[:, None]
    s = jnp.where(live, s, NEG)
    top = jnp.maximum(m, jnp.max(s, axis=-1))
    factor = jnp.exp(m - top)
    weights = jnp.where(live, jnp.exp(s - top[:, None]), 0.0)
    total = l * factor + jnp.sum(weights, axis=-1)
    acc_t = acc * factor[:, None] + jnp.einsum(
        "kj,kjc->kc",
        weights.astype(jnp.bfloat16),
        keys[..., :KVL],
        preferred_element_type=jnp.float32,
    )
    return (acc_t / total[:, None]).astype(jnp.bfloat16)


def join_states(first, second):
    top = jnp.maximum(first[0], second[0])
    f_one = jnp.exp(first[0] - top)
    f_two = jnp.exp(second[0] - top)
    return (
        top,
        first[1] * f_one + second[1] * f_two,
        first[2] * f_one[..., None] + second[2] * f_two[..., None],
    )


def local(
    latent_cache,
    block_owner,
    block_index,
    cache_lengths,
    query_nope,
    query_rope,
    new_latent,
    w_uk,
    value_up_weight,
    w_out,
):
    steps, request_list, heads = (query_nope.shape[0], query_nope.shape[1], query_nope.shape[2])
    q_lat = jnp.einsum(
        "srhn,hnk->srhk", query_nope, w_uk, preferred_element_type=jnp.float32
    ).astype(jnp.bfloat16)
    q_full = jnp.concatenate([q_lat, query_rope], axis=-1)
    picked = jnp.take(q_full, block_owner, axis=1)
    scores = jnp.einsum(
        "sbhc,btc->sbht", picked, latent_cache, preferred_element_type=jnp.float32
    ) * (NOPE + ROPE) ** (-0.5)
    tok_pos = block_index[:, None] * BLK + jnp.arange(BLK, dtype=jnp.int32)[None, :]
    valid = tok_pos < jnp.take(cache_lengths, block_owner)[:, None]
    scores = jnp.where(valid[None, :, None, :], scores, NEG)
    slot_max = jnp.max(scores, axis=-1)
    onehot = block_owner[None, :] == jnp.arange(request_list, dtype=jnp.int32)[:, None]
    req_max = jnp.max(jnp.where(onehot[None, :, :, None], slot_max[:, None], NEG), axis=2)
    slot_top = jnp.take(req_max, block_owner, axis=1)
    weights = jnp.where(valid[None, :, None, :], jnp.exp(scores - slot_top[..., None]), 0.0)
    slot_l = jnp.sum(weights, axis=-1)
    slot_v = jnp.einsum(
        "sbht,btk->sbhk",
        weights.astype(jnp.bfloat16),
        latent_cache[..., :KVL],
        preferred_element_type=jnp.float32,
    )
    mask_f = onehot.astype(jnp.float32)
    req_l = jnp.einsum("rb,sbh->srh", mask_f, slot_l, precision=lax.Precision.HIGHEST)
    req_v = jnp.einsum("rb,sbhk->srhk", mask_f, slot_v, precision=lax.Precision.HIGHEST)
    items = steps * request_list * heads
    width = KVL + ROPE
    m_all, l_all, acc_all = joined((req_max, req_l, req_v), "seq", join_states)
    keys = jnp.broadcast_to(
        jnp.transpose(new_latent, (1, 0, 2))[None, :, None],
        (steps, request_list, heads, steps, width),
    )
    step_of = jnp.broadcast_to(
        jnp.arange(steps, dtype=jnp.int32)[:, None, None], (steps, request_list, heads)
    ).reshape(items)
    latent_output = finish(
        m_all.reshape(items),
        l_all.reshape(items),
        acc_all.reshape(items, KVL),
        q_full.reshape(items, width),
        keys.reshape(items, steps, width),
        step_of,
    )
    value_output = jnp.einsum(
        "fiel,elx->fiex",
        latent_output.reshape(steps, request_list, heads, KVL),
        value_up_weight,
        preferred_element_type=jnp.float32,
    ).astype(jnp.bfloat16)
    rows_all = jnp.transpose(value_output, (1, 0, 2, 3)).reshape(request_list, steps, heads * VD)
    reduced_total = lax.psum_scatter(
        jnp.einsum("rsf,fd->rsd", rows_all, w_out, preferred_element_type=jnp.float32),
        "head",
        scatter_dimension=0,
        tiled=True,
    )
    return reduced_total.astype(jnp.bfloat16)


def solution(mesh):
    in_specs = (
        P("seq", None, None),
        P("seq"),
        P("seq"),
        P(),
        P(None, None, "head", None),
        P(None, None, "head", None),
        P(),
        P("head", None, None),
        P("head", None, None),
        P("head", "seq"),
    )
    out_specs = P("head", None, "seq")
    return jax.shard_map(local, mesh=mesh, in_specs=in_specs, out_specs=out_specs, check_vma=False)
```

profile of v0, /device:TPU:1, one launch (start us, length us, event | category | flops | bytes accessed | tf_op | source)
XLA Modules:
  0.0 402.3 jit_solution(8083136180014012371)
XLA Ops:
  10.7 2.4 gather_fusion.1
  14.0 5.3 %fusion.71 = (f32[2,64,16]{2,0,1:T(2,128)S(1)}, f32[2,64,16,64]{3,2,0,1:T(8,128)S(1)}) fusion(bf16[64,64,576]{2,1,0:T(8,128)(2,1)} %param.12, bf16[64,2,16,576]{3,2,1,0:T(8,128)(2,1)} %gather_fusion.1, pred[64]{0:T(512)(128)(4,1)S(1)} %get-tuple-element.91, pred[64,64]{1,0:T(8,128)(4,1)S(1)} %add_compare_fusion), kind=kOutput, calls=%fused_computation.79 | convolution fusion | flops 152565760 | bytes 7614528 | tf_op jit(solution)/shard_map/sbhc,btc->sbht/dot_general | solution.py:73
  20.3 3.0 fusion.13
  23.3 3.9 fusion.18
  27.2 1.6 copy.72
  28.8 45.5 %all-gather = f32[64,16,16]{2,1,0:T(8,128)S(1)} all-gather(f32[2,16,16]{2,1,0:T(8,128)S(1)} %select_reduce_fusion), channel_id=2, replica_groups=mesh['seq'=32,'head'=8] {'seq'}, dimensions={0}, use_global_device_ids=true | all-gather | bytes 67584 | tf_op jit(solution)/shard_map/all_gather | solution.py:17
  76.2 39.7 %all-gather.1 = f32[64,16,16]{2,1,0:T(8,128)S(1)} all-gather(f32[2,16,16]{2,1,0:T(8,128)S(1)} %copy.70), channel_id=3, replica_groups=mesh['seq'=32,'head'=8] {'seq'}, dimensions={0}, use_global_device_ids=true | all-gather | bytes 67584 | tf_op jit(solution)/shard_map/all_gather | solution.py:17
  117.5 3.1 fusion.27
  122.1 148.0 %all-gather.5.cloned.1.call-done = f32[64,16,16,512]{3,2,1,0:T(8,128)} async-done(((f32[2,16,16,512]{3,2,1,0:T(8,128)}), f32[64,16,16,512]{3,2,1,0:T(8,128)}) %all-gather.5.cloned.1.call-update) | async-done | bytes 33554448 | tf_op jit(solution)/shard_map/all_gather | solution.py:17
  270.0 23.9 %slice.49 = f32[62,16,16,512]{3,2,1,0:T(8,128)} slice(f32[64,16,16,512]{3,2,1,0:T(8,128)} %all-gather.5.cloned.1.call-done), slice={[2:64], [0:16], [0:16], [0:512]} | slice | bytes 65011712 | tf_op jit(solution)/shard_map/slice | solution.py:19
  294.0 71.1 %while.14 = (s32[]{:T(128)}, f32[2,16,16]{2,1,0:T(8,128)S(1)}, f32[2,16,16]{2,1,0:T(8,128)S(1)}, f32[2,16,16,512]{3,2,1,0:T(8,128)S(1)}, f32[31,2,16,16]{3,2,1,0...) while((s32[]{:T(128)}, f32[2,16,16]{2,1,0:T(8,128)S(1)}, ...), condition=%wide.region_4.5_spmd, body=%wide.region_3.4_spmd.sunk | while | flops 789506 | bytes 3166309 | solution.py:20
  299.3 1.5 fusion.80
  301.6 1.5 fusion.80
  310.8 1.5 fusion.80
  313.1 1.5 fusion.80
  322.2 1.5 fusion.80
  333.7 1.5 fusion.80
  342.9 1.5 fusion.80
  345.2 1.5 fusion.80
  354.4 1.5 fusion.80
  365.4 2.2 fusion.47
  367.7 1.8 fusion.46
  369.5 2.3 fusion.42
  372.1 22.8 %all-reduce = bf16[16,2,224]{2,0,1:T(8,128)(2,1)S(1)} all-reduce(f32[16,2,224]{2,0,1:T(8,128)S(1)} %fusion.49), channel_id=5, replica_groups=mesh['seq'=32,'head'=8] {'head'}, use_global_device_ids=true, to_apply=%region_7.8.clone | all-reduce | flops 7168 | bytes 43008
  (113 shorter events, 68.5 us)
Async XLA Ops:
  6.5 3.4 copy-start
  6.5 263.5 %all-gather.5.cloned.1.call-start = ((), (), s32[]{:S(2)}) async-start(), calls=%async_computation | async-start | bytes 34603008 | tf_op jit(solution)/shard_map/all_gather | solution.py:17
  10.7 2.4 copy-start.2
  10.7 3.2 copy-start.5
  10.7 3.2 copy-start.6
  28.8 88.0 %copy-start.4 = (bf16[2,16,576]{2,1,0:T(8,128)(2,1)S(1)}, bf16[2,16,576]{2,1,0:T(8,128)(2,1)}, u32[]{:S(2)}) copy-start(bf16[2,16,576]{2,1,0:T(8,128)(2,1)} %param.18) | copy-start | bytes 110596
  117.5 3.3 copy-start.7
  270.0 23.9 %slice-start = ((f32[64,16,16,512]{3,2,1,0:T(8,128)}), f32[2,16,16,512]{3,2,1,0:T(8,128)S(1)}, s32[]{:S(2)}) async-start(f32[64,16,16,512]{3,2,1,0:T(8,128)} %all-gather.5.cloned.1.call-done), calls=%async_computation.1 | async-start | bytes 2097152 | tf_op jit(solution)/shard_map/slice | solution.py:18
  367.7 27.8 %copy-start.1 = (bf16[16,128,512]{2,1,0:T(8,128)(2,1)S(1)}, bf16[16,128,512]{2,1,0:T(8,128)(2,1)}, u32[]{:S(2)}) copy-start(bf16[16,128,512]{2,1,0:T(8,128)(2,1)} %param.19) | copy-start | bytes 6291460
  367.7 4.1 %copy-start.3 = (bf16[2048,224]{0,1:T(8,128)(2,1)S(1)}, bf16[2048,224]{0,1:T(8,128)(2,1)}, u32[]{:S(2)}) copy-start(bf16[2048,224]{0,1:T(8,128)(2,1)} %param.21) | copy-start | bytes 2752516
Sparse Core Ops, SparseCore 0:
  28.9 241.0 all-gather.4
where the time goes:
time: 409 us; the launch traced here: 402 us
  waiting for transfers between devices  148 us (36%)
  blocking collectives  108 us (26%)
  other arithmetic  75 us (18%)
  local copies, waits for them, and re-layouts  35.7 us (9%)
  matrix products  20.7 us (5%)
  between operations  14.3 us (3%)
    all_gather x1, waiting for transfers between devices, joined(): pieces = jax.tree.map(lambda part: lax.all_gather(part, axis), value)  148 us
    all_gather x2, blocking collectives, joined(): pieces = jax.tree.map(lambda part: lax.all_gather(part, axis), value)  85.2 us
    add x31, other arithmetic, join_states(): first[2] * f_one[..., None] + second[2] * f_two[..., None]  46.8 us
    slice x3, local copies, waits for them, and re-layouts, joined(): tail = jax.tree.map(lambda part: part[1:], pieces)  25.6 us
    add x31, other arithmetic, join_states(): first[1] * f_one + second[1] * f_two  23.6 us
    unnamed x1, blocking collectives  22.8 us
  transfers between devices with their start and end apart: 1, of which 1 were waited for; matrix products, arithmetic and copies ran while one was open for 2% of the time, Pallas kernels for 0%

commit v1 on v0

v1 whole, which is shorter than its diff:
```python
import functools
import math

import jax
import jax.numpy as jnp
from jax import lax
from jax.experimental import pallas as pl
from jax.experimental.pallas import tpu as pltpu
from jax.sharding import PartitionSpec as P

KVL = 512
ROPE = 64
NOPE = 128
VD = 128
BLK = 64
LANES = 128
PITCH = 24

NEG = -1e30
SCALE = (NOPE + ROPE) ** (-0.5) * math.log2(math.e)
VMEM_LIMIT = 48 * 1024 * 1024
GROUP = 8

NT = (((1,), (1,)), ((), ()))


def attend(
    owner,
    index,
    lengths,
    query_nope,
    query_rope,
    new_latent,
    w_uk_hbm,
    value_up_hbm,
    cache_hbm,
    out,
    w_uk,
    value_up,
    cache,
    nope,
    q_lat,
    q_full,
    scores,
    best,
    top,
    part,
    acc,
    message,
    weight_sem,
    cache_sem,
):
    blocks = cache.shape[0]
    steps, requests, heads = query_nope.shape[:3]
    rows = steps * requests
    group = min(GROUP, blocks)
    chunks = blocks // group
    mine = lax.axis_index("seq")

    copy_uk = pltpu.make_async_copy(w_uk_hbm, w_uk, weight_sem.at[0])
    copy_up = pltpu.make_async_copy(value_up_hbm, value_up, weight_sem.at[1])

    def copy_chunk(i):
        span = pl.ds(i * group, group)
        return pltpu.make_async_copy(cache_hbm.at[span], cache.at[span], cache_sem.at[i])

    copy_uk.start()
    for i in range(chunks):
        copy_chunk(i).start()
    copy_up.start()

    nope[...] = query_nope[...].reshape(rows * heads, NOPE).astype(jnp.float32)
    best[...] = jnp.full(best.shape, NEG, jnp.float32)
    part[...] = jnp.zeros(part.shape, jnp.float32)
    acc[...] = jnp.zeros(acc.shape, jnp.float32)
    message[...] = jnp.zeros(message.shape, jnp.float32)

    copy_uk.wait()
    for h in range(heads):
        y = jnp.dot(
            nope[pl.ds(h, rows, stride=heads), :].astype(jnp.bfloat16),
            w_uk[h],
            preferred_element_type=jnp.float32,
        )
        for c in range(KVL // LANES):
            q_lat[c, pl.ds(h, rows, stride=heads), :] = y[:, c * LANES : (c + 1) * LANES]
    for r in range(requests):
        for s in range(steps):
            for c in range(KVL // LANES):
                q_full[r, s * heads : (s + 1) * heads, c * LANES : (c + 1) * LANES] = q_lat[
                    c, (s * requests + r) * heads : (s * requests + r + 1) * heads, :
                ].astype(jnp.bfloat16)
            q_full[r, s * heads : (s + 1) * heads, KVL:] = query_rope[s, r]

    lane = lax.broadcasted_iota(jnp.int32, (steps * heads, BLK), 1)

    def score_chunk(i, carry):
        copy_chunk(i).wait()
        for j in range(group):
            b = i * group + j
            o = owner[b]
            live = lengths[o] - index[b] * BLK
            s = lax.dot_general(q_full[o], cache[b], NT, preferred_element_type=jnp.float32)
            s = jnp.where(lane < live, s * SCALE, NEG)
            scores[b] = s
            best[o] = jnp.maximum(best[o], s)
        return carry

    lax.fori_loop(0, chunks, score_chunk, 0)

    taken = jnp.minimum(mine, requests - 1)
    shape = (steps * heads, steps * requests)
    token = lax.broadcasted_iota(jnp.int32, shape, 1)
    step = lax.broadcasted_iota(jnp.int32, shape, 0) // heads
    allowed = (token % requests == mine) & (token // requests <= step)
    keys = new_latent[...].reshape(steps * requests, KVL + ROPE)
    fresh = lax.dot_general(q_full[taken], keys, NT, preferred_element_type=jnp.float32)
    fresh = jnp.where(allowed, fresh * SCALE, NEG)
    best[taken, :, : steps * requests] = jnp.maximum(best[taken, :, : steps * requests], fresh)

    m = jnp.max(best[...], axis=-1, keepdims=True)
    high = m.astype(jnp.bfloat16).astype(jnp.float32)
    low = (m - high).astype(jnp.bfloat16).astype(jnp.float32)
    top[...] = jnp.broadcast_to(high + low, top.shape)

    def add(o, weights, values):
        y = jnp.dot(weights.astype(jnp.bfloat16), values, preferred_element_type=jnp.float32)
        span = pl.ds(pl.multiple_of(o * (steps * heads), steps * heads), steps * heads)
        for c in range(KVL // LANES):
            acc[c, span, :] += y[:, c * LANES : (c + 1) * LANES]

    def add_chunk(i, carry):
        for j in range(group):
            b = i * group + j
            o = owner[b]
            weights = jnp.exp2(scores[b] - top[o, :, :BLK])
            part[o] += weights
            add(o, weights, cache[b, :, :KVL])
        return carry

    lax.fori_loop(0, chunks, add_chunk, 0)
    weights = jnp.where(allowed, jnp.exp2(fresh - top[taken, :, : steps * requests]), 0.0)
    part[taken, :, : steps * requests] += weights
    add(taken, weights, keys[:, :KVL])

    total = jnp.sum(part[...], axis=-1, keepdims=True)
    best_rows = jnp.broadcast_to(total, top.shape).reshape(rows * heads, LANES)
    nope[...] = best_rows
    q_lat[0] = top[...].reshape(rows * heads, LANES)
    place = lax.broadcasted_iota(jnp.int32, (rows, LANES), 1)
    m_of = jnp.zeros((rows, LANES), jnp.float32)
    l_of = jnp.zeros((rows, LANES), jnp.float32)
    copy_up.wait()
    for h in range(heads):
        every = pl.ds(h, rows, stride=heads)
        x = jnp.concatenate([acc[c, every, :].astype(jnp.bfloat16) for c in range(KVL // LANES)], axis=-1)
        y = jnp.dot(x, value_up[h], preferred_element_type=jnp.float32)
        message[pl.ds(h, rows, stride=PITCH), :] = y
        m_of = jnp.where(place % heads == h, q_lat[0, every, :], m_of)
        l_of = jnp.where(place % heads == h, nope[every, :], l_of)
    m_high = m_of.astype(jnp.bfloat16).astype(jnp.float32)
    l_high = l_of.astype(jnp.bfloat16).astype(jnp.float32)
    kind = place // heads
    state = jnp.where(kind == 0, m_high, jnp.where(kind == 1, m_of - m_high, jnp.where(kind == 2, l_high, l_of - l_high)))
    message[pl.ds(heads, rows, stride=PITCH), :] = state
    out[...] = message[...].reshape(out.shape).astype(jnp.bfloat16)


def combine(parts, out, wide):
    count, pitch, _ = parts.shape
    heads = out.shape[1]
    wide[...] = parts[...].astype(jnp.float32).reshape(wide.shape)
    state = wide[pl.ds(heads, count, stride=pitch), :]
    joined = state + pltpu.roll(state, LANES - heads, 1)
    total = pltpu.roll(joined, LANES - 2 * heads, 1)
    place = lax.broadcasted_iota(jnp.int32, (count, LANES), 1)
    m = jnp.where(place < heads, joined, 0.0)
    l = jnp.where(place < heads, total, 1.0)
    factor = jnp.exp2(m - jnp.max(m, axis=0, keepdims=True))
    share = factor / jnp.sum(factor * l, axis=0, keepdims=True)
    turned = share.T[:heads, :]
    y = jnp.zeros((heads, LANES), jnp.float32)
    for k in range(count):
        y += turned[:, k : k + 1] * wide[pl.ds(k * pitch, heads), :]
    out[...] = jnp.broadcast_to(y.astype(jnp.bfloat16)[None], out.shape)


def project(values, w_out, out, wide):
    rows, heads, _ = values.shape
    wide[...] = values[...].astype(jnp.float32).reshape(wide.shape)
    x = jnp.concatenate(
        [wide[pl.ds(h, rows, stride=heads), :].astype(jnp.bfloat16) for h in range(heads)], axis=-1
    )
    y = jnp.dot(x, w_out[...], preferred_element_type=jnp.float32)
    each = out.shape[1]
    for j in range(out.shape[0]):
        out[j] = y[j * each : (j + 1) * each]


def local(
    head_devices,
    latent_cache,
    block_owner,
    block_index,
    cache_lengths,
    query_nope,
    query_rope,
    new_latent,
    w_uk,
    value_up_weight,
    w_out,
):
    steps, requests, heads = query_nope.shape[:3]
    rows = steps * requests
    blocks = latent_cache.shape[0]
    width = KVL + ROPE
    chunks = blocks // min(GROUP, blocks)
    vmem = pl.BlockSpec(memory_space=pltpu.VMEM)
    smem = pl.BlockSpec(memory_space=pltpu.SMEM)
    hbm = pl.BlockSpec(memory_space=pl.ANY)
    params = pltpu.CompilerParams(vmem_limit_bytes=VMEM_LIMIT)
    f32, bf16 = jnp.float32, jnp.bfloat16
    message = pl.pallas_call(
        attend,
        out_shape=jax.ShapeDtypeStruct((rows, PITCH, LANES), bf16),
        in_specs=[smem, smem, smem, vmem, vmem, vmem, hbm, hbm, hbm],
        out_specs=vmem,
        scratch_shapes=[
            pltpu.VMEM(w_uk.shape, bf16),
            pltpu.VMEM(value_up_weight.shape, bf16),
            pltpu.VMEM(latent_cache.shape, bf16),
            pltpu.VMEM((rows * heads, LANES), f32),
            pltpu.VMEM((KVL // LANES, rows * heads, LANES), f32),
            pltpu.VMEM((requests, steps * heads, width), bf16),
            pltpu.VMEM((blocks, steps * heads, BLK), f32),
            pltpu.VMEM((requests, steps * heads, BLK), f32),
            pltpu.VMEM((requests, steps * heads, LANES), f32),
            pltpu.VMEM((requests, steps * heads, BLK), f32),
            pltpu.VMEM((KVL // LANES, rows * heads, LANES), f32),
            pltpu.VMEM((rows * PITCH, LANES), f32),
            pltpu.SemaphoreType.DMA((2,)),
            pltpu.SemaphoreType.DMA((chunks,)),
        ],
        compiler_params=params,
        name="attend",
    )(
        block_owner,
        block_index,
        cache_lengths,
        query_nope,
        query_rope,
        new_latent,
        w_uk,
        value_up_weight,
        latent_cache,
    )
    parts = lax.all_to_all(message, "seq", 0, 0, tiled=True)
    value = pl.pallas_call(
        combine,
        out_shape=jax.ShapeDtypeStruct((rows, heads, VD), bf16),
        in_specs=[vmem],
        out_specs=vmem,
        scratch_shapes=[pltpu.VMEM((rows * PITCH, LANES), f32)],
        compiler_params=params,
        name="combine",
    )(parts)
    values = lax.all_to_all(value, "seq", 0, 0, tiled=True)
    sums = pl.pallas_call(
        project,
        out_shape=jax.ShapeDtypeStruct((head_devices, rows // head_devices, w_out.shape[1]), f32),
        in_specs=[vmem, vmem],
        out_specs=vmem,
        scratch_shapes=[pltpu.VMEM((rows * heads, LANES), f32)],
        compiler_params=params,
        name="project",
    )(values, w_out)
    sums = lax.all_to_all(sums, "head", 0, 0, tiled=True)
    return jnp.sum(sums, axis=0).reshape(requests // head_devices, steps, w_out.shape[1]).astype(bf16)


def solution(mesh):
    in_specs = (
        P("seq", None, None),
        P("seq"),
        P("seq"),
        P(),
        P(None, None, "head", None),
        P(None, None, "head", None),
        P(),
        P("head", None, None),
        P("head", None, None),
        P("head", "seq"),
    )
    out_specs = P("head", None, "seq")
    body = functools.partial(local, mesh.shape["head"])
    return jax.shard_map(body, mesh=mesh, in_specs=in_specs, out_specs=out_specs, check_vma=False)
```

time: 409 us -> 65.3 us (0.16); the launches traced: 402 us -> 64.9 us
  waiting for transfers between devices: 148 us -> 8.61 us
  blocking collectives: 108 us -> 32.9 us
  other arithmetic: 75 us -> 0.02 us
  local copies, waits for them, and re-layouts: 35.7 us -> 8.85 us
  matrix products: 20.7 us -> 0 us
  between operations: 14.3 us -> 0.04 us
  Pallas kernels: 0 us -> 8.99 us
  starting transfers between devices: 0.01 us -> 5.45 us
    all_gather x1 -> x0, waiting for transfers between devices: 148 us -> none  [joined(): pieces = jax.tree.map(lambda part: lax.all_gather(part, axis), value)]
    all_gather x2 -> x0, blocking collectives: 85.2 us -> none  [joined(): pieces = jax.tree.map(lambda part: lax.all_gather(part, axis), value)]
    add x63 -> x0, other arithmetic: 70.4 us -> none  [the longest x31 46.8 us: join_states(): first[2] * f_one[..., None] + second[2] * f_two[..., None]]
    all_to_all x0 -> x2, blocking collectives: none -> 32.9 us  [the longest x1 21.1 us: local(): parts = lax.all_to_all(message, 'seq', 0, 0, tiled=True)]
    slice x7 -> x0, local copies, waits for them, and re-layouts: 25.6 us -> none  [the longest x3 25.6 us: joined(): tail = jax.tree.map(lambda part: part[1:], pieces)]
    unnamed x1 -> x0, blocking collectives: 22.8 us -> none
    dot_general x8 -> x0, matrix products: 20.3 us -> none  [the longest x1 5.25 us: local(): jnp.einsum('sbhc,btc->sbht', picked, latent_cache, preferred_element_type...]
    pallas_call x0 -> x3, Pallas kernels: none -> 8.99 us  [the longest x1 7.63 us: local(): pl.pallas_call(attend, out_shape=jax.ShapeDtypeStruct((rows, PITCH, LANES...]
  transfers between devices with their start and end apart: 1 -> 1, of which waited for: 1 -> 1; matrix products, arithmetic and copies ran while one was open for 2% -> 1% of each run, Pallas kernels for 0% -> 0%
where the time goes in v1:
time: 65.3 us; the launch traced here: 64.9 us
  blocking collectives  32.9 us (50%)
  Pallas kernels  8.99 us (14%)
  local copies, waits for them, and re-layouts  8.85 us (14%)
  waiting for transfers between devices  8.61 us (13%)
  starting transfers between devices  5.45 us (8%)
    all_to_all x1, blocking collectives, local(): parts = lax.all_to_all(message, 'seq', 0, 0, tiled=True)  21.1 us
    all_to_all x1, blocking collectives, local(): sums = lax.all_to_all(sums, 'head', 0, 0, tiled=True)  11.8 us
    all_to_all x1, waiting for transfers between devices, local(): values = lax.all_to_all(value, 'seq', 0, 0, tiled=True)  8.61 us
    unnamed x19, local copies, waits for them, and re-layouts  8.25 us
    pallas_call x1, Pallas kernels, local(): pl.pallas_call(attend, out_shape=jax.ShapeDtypeStruct((rows, PITCH, LANES...  7.63 us
    all_to_all x1, starting transfers between devices, local(): values = lax.all_to_all(value, 'seq', 0, 0, tiled=True)  5.45 us
  transfers between devices with their start and end apart: 1, of which 1 were waited for; matrix products, arithmetic and copies ran while one was open for 1% of the time, Pallas kernels for 0%

profile of v1, /device:TPU:1, one launch (start us, length us, event | category | flops | bytes accessed | tf_op | source)
XLA Modules:
  0.0 64.9 jit_solution(918030498234462639)
XLA Ops:
  0.0 0.0 copy-start
  0.0 1.6 %copy-done = bf16[16,128,512]{2,1,0:T(8,128)(2,1)S(1)} copy-done((bf16[16,128,512]{2,1,0:T(8,128)(2,1)S(1)}, bf16[16,128,512]{2,1,0:T(8,128)(2,1)}, u32[]{:S(2)}) %copy-start) | copy-done | bytes 2097176
  1.6 0.0 copy-start.1
  1.6 1.6 %copy-done.1 = bf16[16,512,128]{2,1,0:T(8,128)(2,1)S(1)} copy-done((bf16[16,512,128]{2,1,0:T(8,128)(2,1)S(1)}, bf16[16,512,128]{2,1,0:T(8,128)(2,1)}, u32[]{:S(2)}) %copy-start.1) | copy-done | bytes 2097176
  3.2 0.0 copy-start.2
  3.2 0.9 %copy-done.2 = bf16[2,16,16,128]{3,2,1,0:T(8,128)(2,1)S(1)} copy-done((bf16[2,16,16,128]{3,2,1,0:T(8,128)(2,1)S(1)}, bf16[2,16,16,128]{3,2,1,0:T(8,128)(2,1)}, u32[]{:S(2)}) %copy-start.2) | copy-done | bytes 131096
  4.1 0.0 copy-start.3
  4.1 0.9 %copy-done.3 = bf16[2,16,16,64]{3,2,1,0:T(8,128)(2,1)S(1)} copy-done((bf16[2,16,16,64]{3,2,1,0:T(8,128)(2,1)S(1)}, bf16[2,16,16,64]{3,2,1,0:T(8,128)(2,1)}, u32[]{:S(2)}) %copy-start.3) | copy-done | bytes 65560
  5.0 0.0 copy-start.4
  5.0 0.8 %copy-done.4 = bf16[2,16,576]{2,1,0:T(8,128)(2,1)S(1)} copy-done((bf16[2,16,576]{2,1,0:T(8,128)(2,1)S(1)}, bf16[2,16,576]{2,1,0:T(8,128)(2,1)}, u32[]{:S(2)}) %copy-start.4) | copy-done | bytes 36888
  5.8 0.0 copy-start.5
  5.8 0.7 %copy-done.5 = s32[64]{0:T(128)S(1)} copy-done((s32[64]{0:T(128)S(1)}, s32[64]{0:T(128)}, u32[]{:S(2)}) %copy-start.5) | copy-done | bytes 280
  6.4 0.7 %copy-done.6 = s32[64]{0:T(128)S(1)} copy-done((s32[64]{0:T(128)S(1)}, s32[64]{0:T(128)}, u32[]{:S(2)}) %copy-start.6) | copy-done | bytes 280
  7.1 0.7 %copy-done.7 = s32[16]{0:T(128)S(1)} copy-done((s32[16]{0:T(128)S(1)}, s32[16]{0:T(128)}, u32[]{:S(2)}) %copy-start.7) | copy-done | bytes 88
  7.7 7.6 %attend.1 = bf16[32,24,128]{2,1,0:T(8,128)(2,1)S(1)} custom-call(s32[64]{0:T(128)S(1)} %copy-done.5, s32[64]{0:T(128)S(1)} %copy-done.6, s32[16]{0:T(128)S(1)} %copy-done.7, bf16[2,16,16,128]{3,2,1,0:T(8,128)(2,1)S(1)} %copy-done.2, bf16[2,16,16,64]{3,2,1,0:T(8,128)(2,1)S(1)} %copy-done.3, bf16[2,16,576]{2,1,0:T(8,128)(2,1)S(1)} %copy-done.4, ...), custom_call_target="tpu_custom_call" | custom-call | tf_op jit(solution)/shard_map/attend/pallas_call | solution.py:223
  15.4 21.1 %all_to_all.15.parts = bf16[32,24,128]{2,1,0:T(8,128)(2,1)S(1)} all-to-all(bf16[32,24,128]{2,1,0:T(8,128)(2,1)S(1)} %attend.1), channel_id=1, replica_groups=mesh['seq'=32,'head'=8] {'seq'}, dimensions={0} | all-to-all | bytes 393216 | tf_op jit(solution)/shard_map/all_to_all | solution.py:257
  36.4 1.1 %combine.1 = bf16[32,16,128]{2,1,0:T(8,128)(2,1)} custom-call(bf16[32,24,128]{2,1,0:T(8,128)(2,1)S(1)} %all_to_all.15.parts), custom_call_target="tpu_custom_call" | custom-call | tf_op jit(solution)/shard_map/combine/pallas_call | solution.py:258
  37.5 5.5 %all-to-all-start.1 = ((bf16[32,16,128]{2,1,0:T(8,128)(2,1)}), bf16[32,16,128]{2,1,0:T(8,128)(2,1)S(1)}, u32[]{:S(2)}, u32[]{:S(2)}) async-start(bf16[32,16,128]{2,1,0:T(8,128)(2,1)} %combine.1), calls=%async_computation.1 | async-start | bytes 262144 | tf_op jit(solution)/shard_map/all_to_all | solution.py:267
  43.0 0.0 copy-done.8
  43.0 0.5 copy.11.w_out
  43.5 8.6 %all-to-all-done.1.values = bf16[32,16,128]{2,1,0:T(8,128)(2,1)S(1)} async-done(((bf16[32,16,128]{2,1,0:T(8,128)(2,1)}), bf16[32,16,128]{2,1,0:T(8,128)(2,1)S(1)}, u32[]{:S(2)}, u32[]{:S(2)}) %all-to-all-start.1) | async-done | bytes 131104 | tf_op jit(solution)/shard_map/all_to_all | solution.py:267
  52.1 0.3 project.1
  52.4 11.8 %all_to_all.16 = f32[8,4,224]{2,1,0:T(4,128)S(1)} all-to-all(f32[8,4,224]{2,1,0:T(4,128)S(1)} %project.1), channel_id=1, replica_groups=mesh['seq'=32,'head'=8] {'head'}, dimensions={0} | all-to-all | bytes 57344 | tf_op jit(solution)/shard_map/all_to_all | solution.py:277
  64.3 0.6 convert_element_type.7
  (4 shorter events, 0.0 us)
Async XLA Ops:
  0.0 1.6 %copy-start = (bf16[16,128,512]{2,1,0:T(8,128)(2,1)S(1)}, bf16[16,128,512]{2,1,0:T(8,128)(2,1)}, u32[]{:S(2)}) copy-start(bf16[16,128,512]{2,1,0:T(8,128)(2,1)} %w_uk_hbm.1) | copy-start | bytes 6291460
  1.6 1.6 %copy-start.1 = (bf16[16,512,128]{2,1,0:T(8,128)(2,1)S(1)}, bf16[16,512,128]{2,1,0:T(8,128)(2,1)}, u32[]{:S(2)}) copy-start(bf16[16,512,128]{2,1,0:T(8,128)(2,1)} %value_up_hbm.1) | copy-start | bytes 6291460
  3.2 0.9 %copy-start.2 = (bf16[2,16,16,128]{3,2,1,0:T(8,128)(2,1)S(1)}, bf16[2,16,16,128]{3,2,1,0:T(8,128)(2,1)}, u32[]{:S(2)}) copy-start(bf16[2,16,16,128]{3,2,1,0:T(8,128)(2,1)} %query_nope.1) | copy-start | bytes 393220
  4.1 0.9 %copy-start.3 = (bf16[2,16,16,64]{3,2,1,0:T(8,128)(2,1)S(1)}, bf16[2,16,16,64]{3,2,1,0:T(8,128)(2,1)}, u32[]{:S(2)}) copy-start(bf16[2,16,16,64]{3,2,1,0:T(8,128)(2,1)} %query_rope.1) | copy-start | bytes 196612
  5.0 0.8 %copy-start.4 = (bf16[2,16,576]{2,1,0:T(8,128)(2,1)S(1)}, bf16[2,16,576]{2,1,0:T(8,128)(2,1)}, u32[]{:S(2)}) copy-start(bf16[2,16,576]{2,1,0:T(8,128)(2,1)} %new_latent.1) | copy-start | bytes 110596
  5.8 0.7 %copy-start.5 = (s32[64]{0:T(128)S(1)}, s32[64]{0:T(128)}, u32[]{:S(2)}) copy-start(s32[64]{0:T(128)} %owner.1) | copy-start | bytes 772
  6.4 0.7 %copy-start.6 = (s32[64]{0:T(128)S(1)}, s32[64]{0:T(128)}, u32[]{:S(2)}) copy-start(s32[64]{0:T(128)} %index.1) | copy-start | bytes 772
  7.1 0.7 %copy-start.7 = (s32[16]{0:T(128)S(1)}, s32[16]{0:T(128)}, u32[]{:S(2)}) copy-start(s32[16]{0:T(128)} %lengths.1) | copy-start | bytes 196
  7.7 35.3 %copy-start.8 = (bf16[2048,224]{0,1:T(8,128)(2,1)S(1)}, bf16[2048,224]{0,1:T(8,128)(2,1)}, u32[]{:S(2)}) copy-start(bf16[2048,224]{0,1:T(8,128)(2,1)} %param.19) | copy-start | bytes 2752516
  37.5 14.6 %all-to-all-start.1 = ((bf16[32,16,128]{2,1,0:T(8,128)(2,1)}), bf16[32,16,128]{2,1,0:T(8,128)(2,1)S(1)}, u32[]{:S(2)}, u32[]{:S(2)}) async-start(bf16[32,16,128]{2,1,0:T(8,128)(2,1)} %combine.1), calls=%async_computation.1 | async-start | bytes 262144 | tf_op jit(solution)/shard_map/all_to_all | solution.py:267

commit v2 on v1

--- a/solution.py
+++ b/solution.py
@@ -18,23 +18,30 @@
 
 NEG = -1e30
 SCALE = (NOPE + ROPE) ** (-0.5) * math.log2(math.e)
-VMEM_LIMIT = 48 * 1024 * 1024
-GROUP = 8
+VMEM_LIMIT = 60 * 1024 * 1024
+GROUP = 32
+KEY_PARTS = 4
 
 NT = (((1,), (1,)), ((), ()))
 
 
 def attend(
+    owner_hbm,
+    index_hbm,
+    lengths_hbm,
+    query_nope_hbm,
+    query_rope_hbm,
+    new_latent_hbm,
+    w_uk_hbm,
+    value_up_hbm,
+    cache_hbm,
+    out,
     owner,
     index,
     lengths,
     query_nope,
     query_rope,
     new_latent,
-    w_uk_hbm,
-    value_up_hbm,
-    cache_hbm,
-    out,
     w_uk,
     value_up,
     cache,
@@ -47,36 +54,66 @@
     part,
     acc,
     message,
-    weight_sem,
+    small_sem,
+    key_sem,
+    value_sem,
     cache_sem,
 ):
     blocks = cache.shape[0]
-    steps, requests, heads = query_nope.shape[:3]
+    steps, requests, heads = query_nope_hbm.shape[:3]
     rows = steps * requests
     group = min(GROUP, blocks)
     chunks = blocks // group
     mine = lax.axis_index("seq")
 
-    copy_uk = pltpu.make_async_copy(w_uk_hbm, w_uk, weight_sem.at[0])
-    copy_up = pltpu.make_async_copy(value_up_hbm, value_up, weight_sem.at[1])
+    part_heads = heads // KEY_PARTS
+
+    def copy_small(i, source, target):
+        return pltpu.make_async_copy(source, target, small_sem.at[i])
+
+    copy_nope = copy_small(0, query_nope_hbm, query_nope)
+    others = [
+        copy_small(i + 1, source, target)
+        for i, (source, target) in enumerate(
+            [
+                (owner_hbm, owner),
+                (index_hbm, index),
+                (lengths_hbm, lengths),
+                (query_rope_hbm, query_rope),
+                (new_latent_hbm, new_latent),
+            ]
+        )
+    ]
+
+    def copy_uk(i):
+        span = pl.ds(i * part_heads, part_heads)
+        return pltpu.make_async_copy(w_uk_hbm.at[span], w_uk.at[span], key_sem.at[i])
+
+    copy_up = pltpu.make_async_copy(value_up_hbm, value_up, value_sem)
 
     def copy_chunk(i):
         span = pl.ds(i * group, group)
         return pltpu.make_async_copy(cache_hbm.at[span], cache.at[span], cache_sem.at[i])
 
-    copy_uk.start()
+    copy_nope.start()
+    for i in range(KEY_PARTS):
+        copy_uk(i).start()
+    for copy in others:
+        copy.start()
     for i in range(chunks):
         copy_chunk(i).start()
     copy_up.start()
 
-    nope[...] = query_nope[...].reshape(rows * heads, NOPE).astype(jnp.float32)
     best[...] = jnp.full(best.shape, NEG, jnp.float32)
     part[...] = jnp.zeros(part.shape, jnp.float32)
     acc[...] = jnp.zeros(acc.shape, jnp.float32)
     message[...] = jnp.zeros(message.shape, jnp.float32)
 
-    copy_uk.wait()
+    copy_nope.wait()
+    nope[...] = query_nope[...].reshape(rows * heads, NOPE).astype(jnp.float32)
     for h in range(heads):
+        if h % part_heads == 0:
+            copy_uk(h // part_heads).wait()
         y = jnp.dot(
             nope[pl.ds(h, rows, stride=heads), :].astype(jnp.bfloat16),
             w_uk[h],
@@ -84,6 +121,8 @@
         )
         for c in range(KVL // LANES):
             q_lat[c, pl.ds(h, rows, stride=heads), :] = y[:, c * LANES : (c + 1) * LANES]
+    for copy in others:
+        copy.wait()
     for r in range(requests):
         for s in range(steps):
             for c in range(KVL // LANES):
@@ -130,15 +169,15 @@
             acc[c, span, :] += y[:, c * LANES : (c + 1) * LANES]
 
     def add_chunk(i, carry):
-        for j in range(group):
-            b = i * group + j
+        for j in range(min(64, blocks)):
+            b = i * min(64, blocks) + j
             o = owner[b]
             weights = jnp.exp2(scores[b] - top[o, :, :BLK])
             part[o] += weights
             add(o, weights, cache[b, :, :KVL])
         return carry
 
-    lax.fori_loop(0, chunks, add_chunk, 0)
+    lax.fori_loop(0, blocks // min(64, blocks), add_chunk, 0)
     weights = jnp.where(allowed, jnp.exp2(fresh - top[taken, :, : steps * requests]), 0.0)
     part[taken, :, : steps * requests] += weights
     add(taken, weights, keys[:, :KVL])
@@ -191,10 +230,16 @@
     x = jnp.concatenate(
         [wide[pl.ds(h, rows, stride=heads), :].astype(jnp.bfloat16) for h in range(heads)], axis=-1
     )
-    y = jnp.dot(x, w_out[...], preferred_element_type=jnp.float32)
+    y = lax.dot_general(x, w_out[...], NT, preferred_element_type=jnp.float32)
     each = out.shape[1]
     for j in range(out.shape[0]):
         out[j] = y[j * each : (j + 1) * each]
+
+
+def finish(sums, out):
+    y = jnp.sum(sums[...], axis=0).astype(out.dtype)
+    for r in range(out.shape[0]):
+        out[r] = y[r * out.shape[1] : (r + 1) * out.shape[1]]
 
 
 def local(
@@ -216,16 +261,21 @@
     width = KVL + ROPE
     chunks = blocks // min(GROUP, blocks)
     vmem = pl.BlockSpec(memory_space=pltpu.VMEM)
-    smem = pl.BlockSpec(memory_space=pltpu.SMEM)
-    hbm = pl.BlockSpec(memory_space=pl.ANY)
+    hbm = pl.BlockSpec(memory_space=pltpu.HBM)
     params = pltpu.CompilerParams(vmem_limit_bytes=VMEM_LIMIT)
     f32, bf16 = jnp.float32, jnp.bfloat16
     message = pl.pallas_call(
         attend,
         out_shape=jax.ShapeDtypeStruct((rows, PITCH, LANES), bf16),
-        in_specs=[smem, smem, smem, vmem, vmem, vmem, hbm, hbm, hbm],
+        in_specs=[hbm] * 9,
         out_specs=vmem,
         scratch_shapes=[
+            pltpu.SMEM(block_owner.shape, jnp.int32),
+            pltpu.SMEM(block_index.shape, jnp.int32),
+            pltpu.SMEM(cache_lengths.shape, jnp.int32),
+            pltpu.VMEM(query_nope.shape, bf16),
+            pltpu.VMEM(query_rope.shape, bf16),
+            pltpu.VMEM(new_latent.shape, bf16),
             pltpu.VMEM(w_uk.shape, bf16),
             pltpu.VMEM(value_up_weight.shape, bf16),
             pltpu.VMEM(latent_cache.shape, bf16),
@@ -238,7 +288,9 @@
             pltpu.VMEM((requests, steps * heads, BLK), f32),
             pltpu.VMEM((KVL // LANES, rows * heads, LANES), f32),
             pltpu.VMEM((rows * PITCH, LANES), f32),
-            pltpu.SemaphoreType.DMA((2,)),
+            pltpu.SemaphoreType.DMA((6,)),
+            pltpu.SemaphoreType.DMA((KEY_PARTS,)),
+            pltpu.SemaphoreType.DMA,
             pltpu.SemaphoreType.DMA((chunks,)),
         ],
         compiler_params=params,
@@ -261,7 +313,6 @@
         in_specs=[vmem],
         out_specs=vmem,
         scratch_shapes=[pltpu.VMEM((rows * PITCH, LANES), f32)],
-        compiler_params=params,
         name="combine",
     )(parts)
     values = lax.all_to_all(value, "seq", 0, 0, tiled=True)
@@ -271,11 +322,16 @@
         in_specs=[vmem, vmem],
         out_specs=vmem,
         scratch_shapes=[pltpu.VMEM((rows * heads, LANES), f32)],
-        compiler_params=params,
         name="project",
-    )(values, w_out)
+    )(values, w_out.T)
     sums = lax.all_to_all(sums, "head", 0, 0, tiled=True)
-    return jnp.sum(sums, axis=0).reshape(requests // head_devices, steps, w_out.shape[1]).astype(bf16)
+    return pl.pallas_call(
+        finish,
+        out_shape=jax.ShapeDtypeStruct((requests // head_devices, steps, w_out.shape[1]), bf16),
+        in_specs=[vmem],
+        out_specs=vmem,
+        name="finish",
+    )(sums)
 
 
 def solution(mesh):

time: 65.3 us -> 62 us (0.949)
  blocking collectives: 32.9 us -> 48.4 us
  local copies, waits for them, and re-layouts: 8.85 us -> 0 us
  waiting for transfers between devices: 8.61 us -> 0 us
  starting transfers between devices: 5.45 us -> 0 us
  Pallas kernels: 8.99 us -> 13.1 us
    all_to_all x0 -> x1, blocking collectives: none -> 14.7 us  [local(): values = lax.all_to_all(value, 'seq', 0, 0, tiled=True)]
    all_to_all x1 -> x0, waiting for transfers between devices: 8.61 us -> none  [local(): values = lax.all_to_all(value, 'seq', 0, 0, tiled=True)]
    unnamed x19 -> x0, local copies, waits for them, and re-layouts: 8.25 us -> none
    all_to_all x1 -> x0, starting transfers between devices: 5.45 us -> none  [local(): values = lax.all_to_all(value, 'seq', 0, 0, tiled=True)]
    pallas_call x1, Pallas kernels: 0.27 us -> 2.25 us  [local(): pl.pallas_call(project, out_shape=jax.ShapeDtypeStruct((head_devices, row...]
    pallas_call x0 -> x1, Pallas kernels: none -> 1.35 us  [local(): pl.pallas_call(finish, out_shape=jax.ShapeDtypeStruct((requests // head_d...]
    pallas_call x1, Pallas kernels: 1.09 us -> 2.01 us  [local(): pl.pallas_call(combine, out_shape=jax.ShapeDtypeStruct((rows, heads, VD),...]
  transfers between devices with their start and end apart: 1 -> 0, of which waited for: 1 -> 0; matrix products, arithmetic and copies ran while one was open for 1% -> 0% of each run, Pallas kernels for 0% -> 0%
where the time goes in v2:
time: 62 us; the launch traced here: 61.6 us
  blocking collectives  48.4 us (78%)
  Pallas kernels  13.1 us (21%)
    all_to_all x1, blocking collectives, local(): parts = lax.all_to_all(message, 'seq', 0, 0, tiled=True)  21.4 us
    all_to_all x1, blocking collectives, local(): values = lax.all_to_all(value, 'seq', 0, 0, tiled=True)  14.7 us
    all_to_all x1, blocking collectives, local(): sums = lax.all_to_all(sums, 'head', 0, 0, tiled=True)  12.4 us
    pallas_call x1, Pallas kernels, local(): pl.pallas_call(attend, out_shape=jax.ShapeDtypeStruct((rows, PITCH, LANES...  7.52 us
    pallas_call x1, Pallas kernels, local(): pl.pallas_call(project, out_shape=jax.ShapeDtypeStruct((head_devices, row...  2.25 us
    pallas_call x1, Pallas kernels, local(): pl.pallas_call(combine, out_shape=jax.ShapeDtypeStruct((rows, heads, VD),...  2.01 us
    pallas_call x1, Pallas kernels, local(): pl.pallas_call(finish, out_shape=jax.ShapeDtypeStruct((requests // head_d...  1.35 us

profile of v2, /device:TPU:1, one launch (start us, length us, event | category | flops | bytes accessed | tf_op | source)
XLA Modules:
  0.0 61.6 jit_solution(14432446089782128623)
XLA Ops:
  0.0 7.5 %attend.1 = bf16[32,24,128]{2,1,0:T(8,128)(2,1)} custom-call(s32[64]{0:T(128)} %owner_hbm.1, s32[64]{0:T(128)} %index_hbm.1, s32[16]{0:T(128)} %lengths_hbm.1, bf16[2,16,16,128]{3,2,1,0:T(8,128)(2,1)} %query_nope_hbm.1, bf16[2,16,16,64]{3,2,1,0:T(8,128)(2,1)} %query_rope_hbm.1, bf16[2,16,576]{2,1,0:T(8,128)(2,1)} %new_latent_hbm.1, ...), custom_call_target="tpu_custom_call" | custom-call | tf_op jit(solution)/shard_map/attend/pallas_call | solution.py:267
  7.5 21.4 %all_to_all.15.parts = bf16[32,24,128]{2,1,0:T(8,128)(2,1)} all-to-all(bf16[32,24,128]{2,1,0:T(8,128)(2,1)} %attend.1), channel_id=1, replica_groups=mesh['seq'=32,'head'=8] {'seq'}, dimensions={0} | all-to-all | bytes 393216 | tf_op jit(solution)/shard_map/all_to_all | solution.py:309
  28.9 2.0 %combine.1 = bf16[32,16,128]{2,1,0:T(8,128)(2,1)} custom-call(bf16[32,24,128]{2,1,0:T(8,128)(2,1)} %all_to_all.15.parts), custom_call_target="tpu_custom_call" | custom-call | tf_op jit(solution)/shard_map/combine/pallas_call | solution.py:310
  30.9 14.7 %all_to_all.16.values = bf16[32,16,128]{2,1,0:T(8,128)(2,1)} all-to-all(bf16[32,16,128]{2,1,0:T(8,128)(2,1)} %combine.1), channel_id=1, replica_groups=mesh['seq'=32,'head'=8] {'seq'}, dimensions={0} | all-to-all | bytes 262144 | tf_op jit(solution)/shard_map/all_to_all | solution.py:318
  45.6 2.3 %project.1 = f32[8,4,224]{2,1,0:T(4,128)} custom-call(bf16[32,16,128]{2,1,0:T(8,128)(2,1)} %all_to_all.16.values, bf16[224,2048]{1,0:T(8,128)(2,1)} %bitcast.1), custom_call_target="tpu_custom_call" | custom-call | tf_op jit(solution)/shard_map/project/pallas_call | solution.py:319
  47.9 12.4 %all_to_all.17.sums = f32[8,4,224]{2,1,0:T(4,128)} all-to-all(f32[8,4,224]{2,1,0:T(4,128)} %project.1), channel_id=1, replica_groups=mesh['seq'=32,'head'=8] {'head'}, dimensions={0} | all-to-all | bytes 57344 | tf_op jit(solution)/shard_map/all_to_all | solution.py:327
  60.2 1.3 %finish.1 = bf16[2,2,224]{2,1,0:T(2,128)(2,1)} custom-call(f32[8,4,224]{2,1,0:T(4,128)} %all_to_all.17.sums), custom_call_target="tpu_custom_call" | custom-call | tf_op jit(solution)/shard_map/finish/pallas_call | solution.py:328

commit v3 on v2

--- a/solution.py
+++ b/solution.py
@@ -18,7 +18,8 @@
 
 NEG = -1e30
 SCALE = (NOPE + ROPE) ** (-0.5) * math.log2(math.e)
-VMEM_LIMIT = 60 * 1024 * 1024
+VMEM_LIMIT = 48 * 1024 * 1024
+SMALL_LIMIT = 16 * 1024 * 1024
 GROUP = 32
 KEY_PARTS = 4
 
@@ -145,7 +146,8 @@
             best[o] = jnp.maximum(best[o], s)
         return carry
 
-    lax.fori_loop(0, chunks, score_chunk, 0)
+    for i in range(chunks):
+        score_chunk(i, 0)
 
     taken = jnp.minimum(mine, requests - 1)
     shape = (steps * heads, steps * requests)
@@ -266,7 +268,7 @@
     f32, bf16 = jnp.float32, jnp.bfloat16
     message = pl.pallas_call(
         attend,
-        out_shape=jax.ShapeDtypeStruct((rows, PITCH, LANES), bf16),
+        out_shape=pltpu.VMEM((rows, PITCH, LANES), bf16),
         in_specs=[hbm] * 9,
         out_specs=vmem,
         scratch_shapes=[
@@ -296,15 +298,20 @@
         compiler_params=params,
         name="attend",
     )(
-        block_owner,
-        block_index,
-        cache_lengths,
-        query_nope,
-        query_rope,
-        new_latent,
-        w_uk,
-        value_up_weight,
-        latent_cache,
+        *(
+            pltpu.with_memory_space_constraint(x, pltpu.HBM)
+            for x in (
+                block_owner,
+                block_index,
+                cache_lengths,
+                query_nope,
+                query_rope,
+                new_latent,
+                w_uk,
+                value_up_weight,
+                latent_cache,
+            )
+        )
     )
     parts = lax.all_to_all(message, "seq", 0, 0, tiled=True)
     value = pl.pallas_call(
@@ -313,6 +320,7 @@
         in_specs=[vmem],
         out_specs=vmem,
         scratch_shapes=[pltpu.VMEM((rows * PITCH, LANES), f32)],
+        compiler_params=pltpu.CompilerParams(vmem_limit_bytes=SMALL_LIMIT),
         name="combine",
     )(parts)
     values = lax.all_to_all(value, "seq", 0, 0, tiled=True)
@@ -322,6 +330,7 @@
         in_specs=[vmem, vmem],
         out_specs=vmem,
         scratch_shapes=[pltpu.VMEM((rows * heads, LANES), f32)],
+        compiler_params=pltpu.CompilerParams(vmem_limit_bytes=SMALL_LIMIT),
         name="project",
     )(values, w_out.T)
     sums = lax.all_to_all(sums, "head", 0, 0, tiled=True)
@@ -330,6 +339,7 @@
         out_shape=jax.ShapeDtypeStruct((requests // head_devices, steps, w_out.shape[1]), bf16),
         in_specs=[vmem],
         out_specs=vmem,
+        compiler_params=pltpu.CompilerParams(vmem_limit_bytes=SMALL_LIMIT),
         name="finish",
     )(sums)
 

time: 62 us -> 55.7 us (0.90)
  Pallas kernels: 13.1 us -> 8.24 us
  blocking collectives: 48.4 us -> 47.3 us
    pallas_call x1, Pallas kernels: 2.25 us -> 0.39 us  [local(): pl.pallas_call(project, out_shape=jax.ShapeDtypeStruct((head_devices, row...]
    pallas_call x1, Pallas kernels: 2.01 us -> 0.44 us  [local(): pl.pallas_call(combine, out_shape=jax.ShapeDtypeStruct((rows, heads, VD),...]
    pallas_call x1, Pallas kernels: 1.35 us -> 0.59 us  [local(): pl.pallas_call(finish, out_shape=jax.ShapeDtypeStruct((requests // head_d...]
    pallas_call x1, Pallas kernels: 7.52 us -> 6.81 us  [local(): pl.pallas_call(attend, out_shape=pltpu.VMEM((rows, PITCH, LANES), bf16),...]
where the time goes in v3:
time: 55.7 us; the launch traced here: 55.5 us
  blocking collectives  47.3 us (85%)
  Pallas kernels  8.24 us (15%)
    all_to_all x1, blocking collectives, local(): parts = lax.all_to_all(message, 'seq', 0, 0, tiled=True)  21.1 us
    all_to_all x1, blocking collectives, local(): values = lax.all_to_all(value, 'seq', 0, 0, tiled=True)  14.4 us
    all_to_all x1, blocking collectives, local(): sums = lax.all_to_all(sums, 'head', 0, 0, tiled=True)  11.8 us
    pallas_call x1, Pallas kernels, local(): pl.pallas_call(attend, out_shape=pltpu.VMEM((rows, PITCH, LANES), bf16),...  6.81 us

profile of v3, /device:TPU:1, one launch (start us, length us, event | category | flops | bytes accessed | tf_op | source)
XLA Modules:
  0.0 55.5 jit_solution(13290935393426202343)
XLA Ops:
  0.0 0.0 copy-start
  0.0 6.8 %attend.1 = bf16[32,24,128]{2,1,0:T(8,128)(2,1)S(1)} custom-call(s32[64]{0:T(128)} %owner_hbm.1, s32[64]{0:T(128)} %index_hbm.1, s32[16]{0:T(128)} %lengths_hbm.1, bf16[2,16,16,128]{3,2,1,0:T(8,128)(2,1)} %query_nope_hbm.1, bf16[2,16,16,64]{3,2,1,0:T(8,128)(2,1)} %query_rope_hbm.1, bf16[2,16,576]{2,1,0:T(8,128)(2,1)} %new_latent_hbm.1, ...), custom_call_target="tpu_custom_call" | custom-call | tf_op jit(solution)/shard_map/attend/pallas_call | solution.py:269
  6.8 21.1 %all_to_all.15.parts = bf16[32,24,128]{2,1,0:T(8,128)(2,1)S(1)} all-to-all(bf16[32,24,128]{2,1,0:T(8,128)(2,1)S(1)} %attend.1), channel_id=1, replica_groups=mesh['seq'=32,'head'=8] {'seq'}, dimensions={0} | all-to-all | bytes 393216 | tf_op jit(solution)/shard_map/all_to_all | solution.py:316
  27.9 0.4 combine.1
  28.3 14.4 %all_to_all.16.values = bf16[32,16,128]{2,1,0:T(8,128)(2,1)S(1)} all-to-all(bf16[32,16,128]{2,1,0:T(8,128)(2,1)S(1)} %combine.1), channel_id=1, replica_groups=mesh['seq'=32,'head'=8] {'seq'}, dimensions={0} | all-to-all | bytes 262144 | tf_op jit(solution)/shard_map/all_to_all | solution.py:326
  42.7 0.0 copy-done
  42.7 0.4 project.1
  43.1 11.8 %all_to_all.17.sums = f32[8,4,224]{2,1,0:T(4,128)S(1)} all-to-all(f32[8,4,224]{2,1,0:T(4,128)S(1)} %project.1), channel_id=1, replica_groups=mesh['seq'=32,'head'=8] {'head'}, dimensions={0} | all-to-all | bytes 57344 | tf_op jit(solution)/shard_map/all_to_all | solution.py:336
  55.0 0.6 %finish.1 = bf16[2,2,224]{2,1,0:T(2,128)(2,1)} custom-call(f32[8,4,224]{2,1,0:T(4,128)S(1)} %all_to_all.17.sums), custom_call_target="tpu_custom_call" | custom-call | tf_op jit(solution)/shard_map/finish/pallas_call | solution.py:337
Async XLA Ops:
  0.0 42.7 %copy-start = (bf16[2048,224]{0,1:T(8,128)(2,1)S(1)}, bf16[2048,224]{0,1:T(8,128)(2,1)}, u32[]{:S(2)}) copy-start(bf16[2048,224]{0,1:T(8,128)(2,1)} %param.19) | copy-start | bytes 2752516

commit v4 on v3

--- a/solution.py
+++ b/solution.py
@@ -14,7 +14,8 @@
 VD = 128
 BLK = 64
 LANES = 128
-PITCH = 24
+PITCH = 18
+THIN = 2
 
 NEG = -1e30
 SCALE = (NOPE + ROPE) ** (-0.5) * math.log2(math.e)
@@ -208,7 +209,7 @@
 
 
 def combine(parts, out, wide):
-    count, pitch, _ = parts.shape
+    count, pitch = parts.shape[0], PITCH
     heads = out.shape[1]
     wide[...] = parts[...].astype(jnp.float32).reshape(wide.shape)
     state = wide[pl.ds(heads, count, stride=pitch), :]
@@ -268,7 +269,7 @@
     f32, bf16 = jnp.float32, jnp.bfloat16
     message = pl.pallas_call(
         attend,
-        out_shape=pltpu.VMEM((rows, PITCH, LANES), bf16),
+        out_shape=pltpu.VMEM((rows, PITCH // THIN, THIN, LANES), bf16),
         in_specs=[hbm] * 9,
         out_specs=vmem,
         scratch_shapes=[

time: 55.7 us -> 54.7 us (0.982)
  blocking collectives: 47.3 us -> 46.2 us
    all_to_all x1, blocking collectives: 14.4 us -> 13.3 us  [local(): values = lax.all_to_all(value, 'seq', 0, 0, tiled=True)]
where the time goes in v4:
time: 54.7 us; the launch traced here: 54.5 us
  blocking collectives  46.2 us (84%)
  Pallas kernels  8.3 us (15%)
    all_to_all x1, blocking collectives, local(): parts = lax.all_to_all(message, 'seq', 0, 0, tiled=True)  20.9 us
    all_to_all x1, blocking collectives, local(): values = lax.all_to_all(value, 'seq', 0, 0, tiled=True)  13.3 us
    all_to_all x1, blocking collectives, local(): sums = lax.all_to_all(sums, 'head', 0, 0, tiled=True)  11.9 us
    pallas_call x1, Pallas kernels, local(): pl.pallas_call(attend, out_shape=pltpu.VMEM((rows, PITCH // THIN, THIN, L...  6.85 us

profile of v4, /device:TPU:1, one launch (start us, length us, event | category | flops | bytes accessed | tf_op | source)
XLA Modules:
  0.0 54.5 jit_solution(6213082199714162661)
XLA Ops:
  0.0 0.0 copy-start
  0.0 6.8 %attend.1 = bf16[32,9,2,128]{3,2,1,0:T(2,128)(2,1)S(1)} custom-call(s32[64]{0:T(128)} %owner_hbm.1, s32[64]{0:T(128)} %index_hbm.1, s32[16]{0:T(128)} %lengths_hbm.1, bf16[2,16,16,128]{3,2,1,0:T(8,128)(2,1)} %query_nope_hbm.1, bf16[2,16,16,64]{3,2,1,0:T(8,128)(2,1)} %query_rope_hbm.1, bf16[2,16,576]{2,1,0:T(8,128)(2,1)} %new_latent_hbm.1, ...), custom_call_target="tpu_custom_call" | custom-call | tf_op jit(solution)/shard_map/attend/pallas_call | solution.py:270
  6.9 20.9 %all_to_all.15.parts = bf16[32,9,2,128]{3,2,1,0:T(2,128)(2,1)S(1)} all-to-all(bf16[32,9,2,128]{3,2,1,0:T(2,128)(2,1)S(1)} %attend.1), channel_id=1, replica_groups=mesh['seq'=32,'head'=8] {'seq'}, dimensions={0} | all-to-all | bytes 294912 | tf_op jit(solution)/shard_map/all_to_all | solution.py:317
  27.8 0.5 combine.1
  28.3 13.3 %all_to_all.16.values = bf16[32,16,128]{2,1,0:T(8,128)(2,1)S(1)} all-to-all(bf16[32,16,128]{2,1,0:T(8,128)(2,1)S(1)} %combine.1), channel_id=1, replica_groups=mesh['seq'=32,'head'=8] {'seq'}, dimensions={0} | all-to-all | bytes 262144 | tf_op jit(solution)/shard_map/all_to_all | solution.py:327
  41.6 0.0 copy-done
  41.6 0.4 project.1
  42.0 11.9 %all_to_all.17.sums = f32[8,4,224]{2,1,0:T(4,128)S(1)} all-to-all(f32[8,4,224]{2,1,0:T(4,128)S(1)} %project.1), channel_id=1, replica_groups=mesh['seq'=32,'head'=8] {'head'}, dimensions={0} | all-to-all | bytes 57344 | tf_op jit(solution)/shard_map/all_to_all | solution.py:337
  53.9 0.6 %finish.1 = bf16[2,2,224]{2,1,0:T(2,128)(2,1)} custom-call(f32[8,4,224]{2,1,0:T(4,128)S(1)} %all_to_all.17.sums), custom_call_target="tpu_custom_call" | custom-call | tf_op jit(solution)/shard_map/finish/pallas_call | solution.py:338
Async XLA Ops:
  0.0 41.6 %copy-start = (bf16[2048,224]{0,1:T(8,128)(2,1)S(1)}, bf16[2048,224]{0,1:T(8,128)(2,1)}, u32[]{:S(2)}) copy-start(bf16[2048,224]{0,1:T(8,128)(2,1)} %param.19) | copy-start | bytes 2752516

commit v5 on v4

--- a/solution.py
+++ b/solution.py
@@ -37,7 +37,9 @@
     w_uk_hbm,
     value_up_hbm,
     cache_hbm,
+    w_out_hbm,
     out,
+    w_out,
     owner,
     index,
     lengths,
@@ -59,6 +61,7 @@
     small_sem,
     key_sem,
     value_sem,
+    out_sem,
     cache_sem,
 ):
     blocks = cache.shape[0]
@@ -92,6 +95,7 @@
         return pltpu.make_async_copy(w_uk_hbm.at[span], w_uk.at[span], key_sem.at[i])
 
     copy_up = pltpu.make_async_copy(value_up_hbm, value_up, value_sem)
+    copy_out = pltpu.make_async_copy(w_out_hbm, w_out, out_sem)
 
     def copy_chunk(i):
         span = pl.ds(i * group, group)
@@ -105,6 +109,7 @@
     for i in range(chunks):
         copy_chunk(i).start()
     copy_up.start()
+    copy_out.start()
 
     best[...] = jnp.full(best.shape, NEG, jnp.float32)
     part[...] = jnp.zeros(part.shape, jnp.float32)
@@ -206,6 +211,7 @@
     state = jnp.where(kind == 0, m_high, jnp.where(kind == 1, m_of - m_high, jnp.where(kind == 2, l_high, l_of - l_high)))
     message[pl.ds(heads, rows, stride=PITCH), :] = state
     out[...] = message[...].reshape(out.shape).astype(jnp.bfloat16)
+    copy_out.wait()
 
 
 def combine(parts, out, wide):
@@ -267,11 +273,14 @@
     hbm = pl.BlockSpec(memory_space=pltpu.HBM)
     params = pltpu.CompilerParams(vmem_limit_bytes=VMEM_LIMIT)
     f32, bf16 = jnp.float32, jnp.bfloat16
-    message = pl.pallas_call(
+    message, w_out_near = pl.pallas_call(
         attend,
-        out_shape=pltpu.VMEM((rows, PITCH // THIN, THIN, LANES), bf16),
-        in_specs=[hbm] * 9,
-        out_specs=vmem,
+        out_shape=(
+            pltpu.VMEM((rows, PITCH // THIN, THIN, LANES), bf16),
+            pltpu.VMEM(w_out.shape[::-1], bf16),
+        ),
+        in_specs=[hbm] * 10,
+        out_specs=(vmem, vmem),
         scratch_shapes=[
             pltpu.SMEM(block_owner.shape, jnp.int32),
             pltpu.SMEM(block_index.shape, jnp.int32),
@@ -294,6 +303,7 @@
             pltpu.SemaphoreType.DMA((6,)),
             pltpu.SemaphoreType.DMA((KEY_PARTS,)),
             pltpu.SemaphoreType.DMA,
+            pltpu.SemaphoreType.DMA,
             pltpu.SemaphoreType.DMA((chunks,)),
         ],
         compiler_params=params,
@@ -311,6 +321,7 @@
                 w_uk,
                 value_up_weight,
                 latent_cache,
+                w_out.T,
             )
         )
     )
@@ -333,7 +344,7 @@
         scratch_shapes=[pltpu.VMEM((rows * heads, LANES), f32)],
         compiler_params=pltpu.CompilerParams(vmem_limit_bytes=SMALL_LIMIT),
         name="project",
-    )(values, w_out.T)
+    )(values, w_out_near)
     sums = lax.all_to_all(sums, "head", 0, 0, tiled=True)
     return pl.pallas_call(
         finish,

time: 54.7 us -> 54.6 us (level)
  no operation moved by 1% of the time
where the time goes in v5:
time: 54.6 us; the launch traced here: 54.4 us
  blocking collectives  46.2 us (85%)
  Pallas kernels  8.23 us (15%)
    all_to_all x1, blocking collectives, local(): parts = lax.all_to_all(message, 'seq', 0, 0, tiled=True)  21 us
    all_to_all x1, blocking collectives, local(): values = lax.all_to_all(value, 'seq', 0, 0, tiled=True)  13.3 us
    all_to_all x1, blocking collectives, local(): sums = lax.all_to_all(sums, 'head', 0, 0, tiled=True)  11.9 us
    pallas_call x1, Pallas kernels, local(): pl.pallas_call(attend, out_shape=(pltpu.VMEM((rows, PITCH // THIN, THIN,...  6.77 us

profile of v5, /device:TPU:1, one launch (start us, length us, event | category | flops | bytes accessed | tf_op | source)
XLA Modules:
  0.0 54.4 jit_solution(18153372821360704623)
XLA Ops:
  0.0 6.8 %attend.1 = (bf16[32,9,2,128]{3,2,1,0:T(2,128)(2,1)S(1)}, bf16[224,2048]{1,0:T(8,128)(2,1)S(1)}) custom-call(s32[64]{0:T(128)} %owner_hbm.1, s32[64]{0:T(128)} %index_hbm.1, s32[16]{0:T(128)} %lengths_hbm.1, bf16[2,16,16,128]{3,2,1,0:T(8,128)(2,1)} %query_nope_hbm.1, bf16[2,16,16,64]{3,2,1,0:T(8,128)(2,1)} %query_rope_hbm.1, ...), custom_call_target="tpu_custom_call" | custom-call | tf_op jit(solution)/shard_map/attend/pallas_call | solution.py:276
  6.8 21.0 %all_to_all.15.parts = bf16[32,9,2,128]{3,2,1,0:T(2,128)(2,1)S(1)} all-to-all(bf16[32,9,2,128]{3,2,1,0:T(2,128)(2,1)S(1)} %get-tuple-element.7), channel_id=1, replica_groups=mesh['seq'=32,'head'=8] {'seq'}, dimensions={0} | all-to-all | bytes 294912 | tf_op jit(solution)/shard_map/all_to_all | solution.py:328
  27.7 0.5 combine.1
  28.2 13.3 %all_to_all.16.values = bf16[32,16,128]{2,1,0:T(8,128)(2,1)S(1)} all-to-all(bf16[32,16,128]{2,1,0:T(8,128)(2,1)S(1)} %combine.1), channel_id=1, replica_groups=mesh['seq'=32,'head'=8] {'seq'}, dimensions={0} | all-to-all | bytes 262144 | tf_op jit(solution)/shard_map/all_to_all | solution.py:338
  41.5 0.4 project.1
  41.9 11.9 %all_to_all.17.sums = f32[8,4,224]{2,1,0:T(4,128)S(1)} all-to-all(f32[8,4,224]{2,1,0:T(4,128)S(1)} %project.1), channel_id=1, replica_groups=mesh['seq'=32,'head'=8] {'head'}, dimensions={0} | all-to-all | bytes 57344 | tf_op jit(solution)/shard_map/all_to_all | solution.py:348
  53.8 0.6 %finish.1 = bf16[2,2,224]{2,1,0:T(2,128)(2,1)} custom-call(f32[8,4,224]{2,1,0:T(4,128)S(1)} %all_to_all.17.sums), custom_call_target="tpu_custom_call" | custom-call | tf_op jit(solution)/shard_map/finish/pallas_call | solution.py:349

commit v6 on v4

--- a/solution.py
+++ b/solution.py
@@ -236,11 +236,11 @@
     y = lax.dot_general(x, w_out[...], NT, preferred_element_type=jnp.float32)
     each = out.shape[1]
     for j in range(out.shape[0]):
-        out[j] = y[j * each : (j + 1) * each]
+        out[j] = y[j * each : (j + 1) * each].astype(out.dtype)
 
 
 def finish(sums, out):
-    y = jnp.sum(sums[...], axis=0).astype(out.dtype)
+    y = jnp.sum(sums[...].astype(jnp.float32), axis=0).astype(out.dtype)
     for r in range(out.shape[0]):
         out[r] = y[r * out.shape[1] : (r + 1) * out.shape[1]]
 
@@ -327,7 +327,7 @@
     values = lax.all_to_all(value, "seq", 0, 0, tiled=True)
     sums = pl.pallas_call(
         project,
-        out_shape=jax.ShapeDtypeStruct((head_devices, rows // head_devices, w_out.shape[1]), f32),
+        out_shape=jax.ShapeDtypeStruct((head_devices, rows // head_devices, w_out.shape[1]), bf16),
         in_specs=[vmem, vmem],
         out_specs=vmem,
         scratch_shapes=[pltpu.VMEM((rows * heads, LANES), f32)],

time: 54.7 us -> 54.6 us (level)
  no operation moved by 1% of the time
where the time goes in v6:
time: 54.6 us; the launch traced here: 54.5 us
  blocking collectives  46.1 us (84%)
  Pallas kernels  8.29 us (15%)
    all_to_all x1, blocking collectives, local(): parts = lax.all_to_all(message, 'seq', 0, 0, tiled=True)  21 us
    all_to_all x1, blocking collectives, local(): values = lax.all_to_all(value, 'seq', 0, 0, tiled=True)  13.3 us
    all_to_all x1, blocking collectives, local(): sums = lax.all_to_all(sums, 'head', 0, 0, tiled=True)  11.9 us
    pallas_call x1, Pallas kernels, local(): pl.pallas_call(attend, out_shape=pltpu.VMEM((rows, PITCH // THIN, THIN, L...  6.83 us

profile of v6, /device:TPU:1, one launch (start us, length us, event | category | flops | bytes accessed | tf_op | source)
XLA Modules:
  0.0 54.5 jit_solution(5773215363085848994)
XLA Ops:
  0.0 0.0 copy-start
  0.0 6.8 %attend.1 = bf16[32,9,2,128]{3,2,1,0:T(2,128)(2,1)S(1)} custom-call(s32[64]{0:T(128)} %owner_hbm.1, s32[64]{0:T(128)} %index_hbm.1, s32[16]{0:T(128)} %lengths_hbm.1, bf16[2,16,16,128]{3,2,1,0:T(8,128)(2,1)} %query_nope_hbm.1, bf16[2,16,16,64]{3,2,1,0:T(8,128)(2,1)} %query_rope_hbm.1, bf16[2,16,576]{2,1,0:T(8,128)(2,1)} %new_latent_hbm.1, ...), custom_call_target="tpu_custom_call" | custom-call | tf_op jit(solution)/shard_map/attend/pallas_call | solution.py:270
  6.8 21.0 %all_to_all.15.parts = bf16[32,9,2,128]{3,2,1,0:T(2,128)(2,1)S(1)} all-to-all(bf16[32,9,2,128]{3,2,1,0:T(2,128)(2,1)S(1)} %attend.1), channel_id=1, replica_groups=mesh['seq'=32,'head'=8] {'seq'}, dimensions={0} | all-to-all | bytes 294912 | tf_op jit(solution)/shard_map/all_to_all | solution.py:317
  27.8 0.5 combine.1
  28.3 13.3 %all_to_all.16.values = bf16[32,16,128]{2,1,0:T(8,128)(2,1)S(1)} all-to-all(bf16[32,16,128]{2,1,0:T(8,128)(2,1)S(1)} %combine.1), channel_id=1, replica_groups=mesh['seq'=32,'head'=8] {'seq'}, dimensions={0} | all-to-all | bytes 262144 | tf_op jit(solution)/shard_map/all_to_all | solution.py:327
  41.6 0.0 copy-done
  41.6 0.4 project.1
  42.0 11.9 %all_to_all.17.sums = bf16[8,4,224]{2,1,0:T(4,128)(2,1)S(1)} all-to-all(bf16[8,4,224]{2,1,0:T(4,128)(2,1)S(1)} %project.1), channel_id=1, replica_groups=mesh['seq'=32,'head'=8] {'head'}, dimensions={0} | all-to-all | bytes 28672 | tf_op jit(solution)/shard_map/all_to_all | solution.py:337
  53.9 0.6 %finish.1 = bf16[2,2,224]{2,1,0:T(2,128)(2,1)} custom-call(bf16[8,4,224]{2,1,0:T(4,128)(2,1)S(1)} %all_to_all.17.sums), custom_call_target="tpu_custom_call" | custom-call | tf_op jit(solution)/shard_map/finish/pallas_call | solution.py:338
Async XLA Ops:
  0.0 41.6 %copy-start = (bf16[2048,224]{0,1:T(8,128)(2,1)S(1)}, bf16[2048,224]{0,1:T(8,128)(2,1)}, u32[]{:S(2)}) copy-start(bf16[2048,224]{0,1:T(8,128)(2,1)} %param.19) | copy-start | bytes 2752516
